TPU v7x, 512 devices: a whole 4x4x16 slice. The times are simulated.
512 devices in a mesh: ops: 128 (over z, x_hi, y), sec: 4 (over x_lo, core).
Axes of the slice: x: 4 (x_hi: 2, x_lo: 2; x = x_hi * 2 + x_lo), y: 4, z: 16, core: 2. Of those that a mesh axis runs over, the one named last changes fastest.
Arguments:
- wave: bfloat16 [4, 256, 256], P('sec', 'ops'), may hold values from -12 to 12
- sector_live: int32 [4], P('sec'), may hold values from 128 to 256, as said below
- left_ops: bfloat16 [4, 1536, 256, 256], P('sec', 'ops'), may hold values from -24 to 24
- right_ops: bfloat16 [4, 1536, 256, 256], P('sec', 'ops'), may hold values from -0.375 to 0.375
- pair_shift: int32 [1536], P('ops'), may hold values from -2 to 2
- pair_orbitals: int32 [1536, 2], P('ops'), may hold values from 0 to 119
- orbital_scale: float32 [120], replicated, may hold values from 0.5 to 2
- block_ham: bfloat16 [4, 256, 256], P('sec', 'ops'), may hold values from -1 to 4
- site_basis: bfloat16 [4, 256, 256], P('sec', 'ops'), may hold values from -0.375 to 0.375
Outputs:
- residual: float32 [4, 256, 256], P('sec', 'ops')
- renormalized: bfloat16 [4, 1536, 256, 256], P('sec', 'ops')
Inputs may be any that keep to these rules, and one draw needn't show every extreme that they name: `sector_live`: in every draw some sector has all 256 rows live.
All inputs are finite; a program needn't handle non-finite values.
Results may differ from a plain program's by a relative error of at most 0.0049.
Values may be sent and summed in bfloat16 or wider, within the bound.
A program may use at most 64 MiB of HBM per device.

v0:
```python
import math

import jax
import jax.numpy as jnp
from jax import lax
from jax.sharding import PartitionSpec as P

NORB = 120


def fetch_rows(stacked):
    return lax.all_gather(stacked, "ops", axis=1, tiled=True)


def fetch_sectors(stacked):
    return lax.all_gather(stacked, "sec", axis=0, tiled=True)


def on_device(
    wave,
    sector_live,
    left_ops,
    right_ops,
    pair_shift,
    pair_orbitals,
    orbital_scale,
    block_ham,
    site_basis,
):
    row_count = wave.shape[1]
    width = wave.shape[2]
    sector_count = lax.axis_size("sec")
    sector = lax.axis_index("sec")
    row_start = lax.axis_index("ops") * row_count
    row_ids = row_start + lax.iota(jnp.int32, row_count)
    column_ids = lax.iota(jnp.int32, width)
    live_size = sector_live[0]
    keep_mask = (row_ids[:, None] < live_size) & (column_ids[None, :] < live_size)
    masked = jnp.where(keep_mask[None], wave, jnp.zeros_like(wave))
    stacked = jnp.concatenate([masked, site_basis], axis=2)
    fetched = fetch_sectors(fetch_rows(stacked))
    held_count = fetched.shape[0]
    wave_all = fetched[:, :, :width]
    basis_all = fetched[:, :, width:]
    one_hot = (pair_orbitals[:, :, None] == lax.iota(jnp.int32, NORB)[None, None, :]).astype(
        jnp.float32
    )
    scales = jnp.sum(one_hot * orbital_scale[None, None, :], axis=2)
    pair_total = left_ops.shape[1] * lax.axis_size("ops")
    coupling = scales[:, 0] * scales[:, 1] / math.sqrt(width * pair_total)
    source = sector - pair_shift
    in_range = (source >= 0) & (source < sector_count)
    weight_used = jnp.where(in_range, coupling, jnp.zeros_like(coupling))
    local_index = jnp.clip(source, 0, held_count - 1)
    wave_src = wave_all[local_index]
    basis_src = basis_all[local_index]
    wave_own = lax.dynamic_index_in_dim(wave_all, sector, 0, keepdims=False)
    basis_own = lax.dynamic_index_in_dim(basis_all, sector, 0, keepdims=False)
    left_here = left_ops[0]
    product = jnp.einsum("pab,pcb->pac", wave_src, right_ops[0], preferred_element_type=jnp.float32)
    carried = (weight_used[:, None, None] * product).astype(jnp.bfloat16)
    summed = lax.psum_scatter(
        jnp.einsum("pab,pbc->ac", left_here, carried, preferred_element_type=jnp.float32),
        "ops",
        scatter_dimension=0,
        tiled=True,
    )
    sigma = summed + jnp.dot(block_ham[0], wave_own, preferred_element_type=jnp.float32)
    masked_wide = masked[0].astype(jnp.float32)
    correlation, norm_sq = lax.psum(
        (jnp.sum(masked_wide * sigma), jnp.sum(masked_wide * masked_wide)), ("ops", "sec")
    )
    energy = correlation / norm_sq
    residual = sigma - energy * masked_wide
    left_basis = jnp.einsum(
        "pab,pbc->pac", left_here, basis_src, preferred_element_type=jnp.float32
    ).astype(jnp.bfloat16)
    renormed = jnp.einsum("ab,pac->pbc", basis_own, left_basis, preferred_element_type=jnp.float32)
    renormed = jnp.where(in_range[:, None, None], renormed, jnp.zeros_like(renormed)).astype(
        jnp.bfloat16
    )
    return (residual[None], renormed[None])


def solution(mesh):
    placed = (
        P("sec", "ops", None),
        P("sec"),
        P("sec", "ops", None, None),
        P("sec", "ops", None, None),
        P("ops"),
        P("ops", None),
        P(),
        P("sec", "ops", None),
        P("sec", "ops", None),
    )
    return jax.shard_map(
        on_device,
        mesh=mesh,
        in_specs=placed,
        out_specs=(P("sec", "ops", None), P("sec", "ops", None, None)),
        check_vma=False,
    )
```

profile of v0, /device:TPU:1, one launch (start us, length us, event | category | flops | bytes accessed | tf_op | source)
XLA Modules:
  0.0 1738.8 jit_solution(4303738478419335191)
XLA Ops:
  7.2 0.0 copy-start
  7.2 0.0 copy-start.3
  7.2 0.0 copy-start.5
  7.2 0.0 copy-start.4
  7.2 0.0 all-gather.2.cloned.1.call-start
  8.0 0.8 and_select_fusion
  8.8 0.7 pad_maximum_fusion
  9.5 310.0 %all_gather.6 = bf16[1,256,512]{2,0,1:T(2,128)(2,1)S(1)} all-gather(bf16[1,2,512]{2,0,1:T(2,128)(2,1)S(1)} %copy.39), channel_id=1, replica_groups=mesh['ops'=128,'sec'=4] {'ops'}, dimensions={1}, use_global_device_ids=true | all-gather | bytes 264192 | tf_op jit(solution)/shard_map/all_gather | solution.py:12
  319.5 0.7 copy.40
  320.2 0.0 all-gather.2.cloned.1.call-update
  320.2 0.0 all-reduce.4.cloned.1.call-start
  320.3 0.0 copy-done.3
  320.3 0.1 copy.38
  320.4 1.3 dynamic-slice
  322.3 0.0 copy-done.5
  322.4 0.0 copy-done.4
  322.4 0.2 fusion.24
  322.5 0.2 fusion.26
  322.7 71.6 %all-gather.2.cloned.1.call-done = bf16[4,256,512]{2,1,0:T(8,128)(2,1)} async-done(((bf16[1,256,512]{2,1,0:T(8,128)(2,1)}), bf16[4,256,512]{2,1,0:T(8,128)(2,1)}) %all-gather.2.cloned.1.call-update) | async-done | bytes 1048592 | tf_op jit(solution)/shard_map/all_gather | solution.py:16
  394.3 1.3 fusion.34
  395.6 1.8 gather_fusion
  397.4 4.0 fusion.14
  401.5 0.0 all-reduce.4.cloned.1.call-update
  401.5 1.8 gather_fusion.1
  403.3 3.6 fusion.5
  407.0 2.6 copy.44
  409.5 1180.0 %all-reduce.4.cloned.1.call-done = f32[256,256]{0,1:T(8,128)} async-done(((f32[256,256]{0,1:T(8,128)}), f32[256,256]{0,1:T(8,128)}) %all-reduce.4.cloned.1.call-update) | async-done | bytes 262160
  1589.6 1.0 constant_dynamic-slice_fusion
  1590.6 0.1 copy.42
  1590.7 0.8 fusion.28
  1591.5 138.5 %all-reduce.1 = (f32[]{:T(128)}, f32[]{:T(128)}) all-reduce(f32[]{:T(128)} %get-tuple-element.13, f32[]{:T(128)} %get-tuple-element.12), channel_id=1, replica_groups=mesh['ops'=128,'sec'=4] {'ops','sec'}, use_global_device_ids=true, to_apply=%region_3.4 | all-reduce | flops 2 | bytes 16 | tf_op jit(solution)/shard_map/psum | solution.py:70
  1731.3 0.7 fusion.30
  (11 shorter events, 0.1 us)
Async XLA Ops:
  7.2 390.3 %copy-start = (bf16[1,12,256,256]{3,2,1,0:T(8,128)(2,1)S(1)}, bf16[1,12,256,256]{3,2,1,0:T(8,128)(2,1)}, u32[]{:S(2)}) copy-start(bf16[1,12,256,256]{3,2,1,0:T(8,128)(2,1)} %param.11) | copy-start | bytes 4718596
  7.2 313.1 %copy-start.3 = (s32[12,2]{0,1:T(2,128)S(1)}, s32[12,2]{0,1:T(2,128)}, u32[]{:S(2)}) copy-start(s32[12,2]{0,1:T(2,128)} %param.14) | copy-start | bytes 292
  7.2 315.1 %copy-start.5 = (s32[12]{0:T(128)S(1)}, s32[12]{0:T(128)}, u32[]{:S(2)}) copy-start(s32[12]{0:T(128)} %param.13) | copy-start | bytes 148
  7.2 315.2 %copy-start.4 = (f32[120]{0:T(128)S(1)}, f32[120]{0:T(128)}, u32[]{:S(2)}) copy-start(f32[120]{0:T(128)} %param.15) | copy-start | bytes 1444
  7.2 387.1 %all-gather.2.cloned.1.call-start = ((), (), s32[]{:S(2)}) async-start(), calls=%async_computation | async-start | bytes 1310720 | tf_op jit(solution)/shard_map/all_gather | solution.py:16
  320.2 1269.3 %all-reduce.4.cloned.1.call-start = ((), (), s32[]{:S(2)}) async-start(), calls=%async_computation.1 | async-start | bytes 524288
  406.9 1183.7 %copy-start.2 = (bf16[1,2,256]{2,1,0:T(2,128)(2,1)S(1)}, bf16[1,2,256]{2,1,0:T(2,128)(2,1)}, u32[]{:S(2)}) copy-start(bf16[1,2,256]{2,1,0:T(2,128)(2,1)} %param.16) | copy-start | bytes 3076
  406.9 1324.3 %copy-start.1 = (bf16[1,2,256]{2,1,0:T(2,128)(2,1)S(1)}, bf16[1,2,256]{2,1,0:T(2,128)(2,1)}, u32[]{:S(2)}) copy-start(bf16[1,2,256]{2,1,0:T(2,128)(2,1)} %param.9) | copy-start | bytes 3076
Sparse Core Ops, SparseCore 0:
  320.4 73.9 all-gather.1
  401.6 1187.9 all-reduce.3
where the time goes:
time: 1740 us
  waiting for transfers between devices  1250 us (72%)
  blocking collectives  448 us (26%)
    unnamed x3, waiting for transfers between devices  1180 us
    all_gather x1, blocking collectives, fetch_rows(): return lax.all_gather(stacked, 'ops', axis=1, tiled=True)  310 us
    psum x1, blocking collectives, on_device(): lax.psum((jnp.sum(masked_wide * sigma), jnp.sum(masked_wide * masked_wide...  139 us
    all_gather x1, waiting for transfers between devices, fetch_sectors(): return lax.all_gather(stacked, 'sec', axis=0, tiled=True)  71.6 us
  transfers between devices with their start and end apart: 2, of which 2 were waited for; matrix products, arithmetic and copies ran while one was open for 1% of the time, Pallas kernels for 0%

commit v1 on v0

v1 whole, which is shorter than its diff:
```python
import functools
import math

import jax
import jax.numpy as jnp
from jax import lax
from jax.experimental import pallas as pl
from jax.experimental.pallas import tpu as pltpu
from jax.sharding import PartitionSpec as P

MESH = pl.DeviceIdType.MESH
F32 = jnp.float32
BF16 = jnp.bfloat16
NZ = 16
NJ = 8
NX = 16
NSEC = 4
NPAIR = 12
D = 256
H = 128
SCALE = 1.0 / math.sqrt(256 * 1536)


def nt(a, b):
    return lax.dot_general(a, b, (((1,), (1,)), ((), ())), preferred_element_type=F32)


def nn(a, b):
    return jnp.dot(a, b, preferred_element_type=F32)


def kernel(
    live_ref,
    shift_ref,
    orb_ref,
    scale_ref,
    wave_ref,
    ham_ref,
    basis_ref,
    left_hbm,
    right_hbm,
    resid_ref,
    renorm_hbm,
    left,
    right,
    carried,
    renorm,
    zbuf,
    wall,
    mats,
    perm,
    basis_t,
    sig,
    rs_send,
    rs_recv,
    corr_own,
    corr_sib,
    corr_x,
    zs_send,
    zs_recv,
    load_sem,
    out_sem,
    zsend_sem,
    zrecv_sem,
    xsend_sem,
    xrecv_sem,
    csend_sem,
    crecv_sem,
    rsend_sem,
    rrecv_sem,
    ksend_sem,
    krecv_sem,
    qsend_sem,
    qrecv_sem,
    ssend_sem,
    srecv_sem,
):
    ops = lax.axis_index("ops")
    sec = lax.axis_index("sec")
    z = ops // NJ
    j = ops % NJ
    x_lo = sec // 2
    core = sec % 2
    plane = x_lo * NJ + j

    def at_z(i):
        return {"ops": lax.rem(z + i, NZ) * NJ + j, "sec": sec}

    def at_plane(i):
        p = lax.rem(plane + i, NX)
        return {"ops": z * NJ + p % NJ, "sec": (p // NJ) * 2 + core}

    sibling = {"ops": ops, "sec": x_lo * 2 + (1 - core)}

    def remote(src, dst, send, recv, device):
        return pltpu.make_async_remote_copy(
            src_ref=src, dst_ref=dst, send_sem=send, recv_sem=recv, device_id=device, device_id_type=MESH
        )

    def taken(ref, sem):
        pltpu.make_async_copy(ref, ref, sem).wait()

    for k in range(NPAIR):
        pltpu.make_async_copy(right_hbm.at[0, k], right.at[k], load_sem.at[0]).start()
    for k in range(NPAIR):
        pltpu.make_async_copy(left_hbm.at[0, k], left.at[k], load_sem.at[1]).start()

    barrier = pltpu.get_barrier_semaphore()

    def greet_z(i, _):
        pl.semaphore_signal(barrier, inc=1, device_id=at_z(i), device_id_type=MESH)
        return 0

    def greet_plane(i, _):
        pl.semaphore_signal(barrier, inc=1, device_id=at_plane(i), device_id_type=MESH)
        return 0

    lax.fori_loop(1, NZ, greet_z, 0)
    lax.fori_loop(1, NX, greet_plane, 0)
    pl.semaphore_signal(barrier, inc=1, device_id=sibling, device_id_type=MESH)

    live = live_ref[0]
    row_ids = ops * 2 + lax.broadcasted_iota(jnp.int32, (2, D), 0)
    col_ids = lax.broadcasted_iota(jnp.int32, (2, D), 1)
    keep = (row_ids < live) & (col_ids < live)
    masked_rows = jnp.where(keep, wave_ref[0].astype(F32), 0.0)
    basis_rows = basis_ref[0].astype(F32)
    for h in range(2):
        zbuf[0, z, 2 * h : 2 * h + 2, :] = masked_rows[:, h * H : (h + 1) * H]
        zbuf[1, z, 2 * h : 2 * h + 2, :] = basis_rows[:, h * H : (h + 1) * H]

    m_ids = lax.broadcasted_iota(jnp.int32, (D, D), 0)
    s_ids = lax.broadcasted_iota(jnp.int32, (D, D), 1)
    wanted = ((m_ids % 16) // 2) * 32 + (m_ids % 2) * 16 + m_ids // 16
    perm[0] = jnp.where(wanted == s_ids, 1.0, 0.0).astype(BF16)
    perm[1] = jnp.where(m_ids == s_ids, 1.0, 0.0).astype(BF16)

    pl.semaphore_wait(barrier, (NZ - 1) + (NX - 1) + 1)

    for w in range(2):

        def send_z(i, _):
            remote(
                zbuf.at[w, z], zbuf.at[w, z], zsend_sem.at[w], zrecv_sem.at[w], at_z(i)
            ).start()
            return 0

        lax.fori_loop(1, NZ, send_z, 0)

    slot = sec * NJ + j
    for w in range(2):
        taken(zbuf.at[w, pl.ds(0, NZ - 1)], zrecv_sem.at[w])
        for h in range(2):
            for r in range(2):
                wall[w, slot, r * 16 : (r + 1) * 16, h * H : (h + 1) * H] = zbuf[w, :, 2 * h + r, :].astype(BF16)

        def send_plane(i, _):
            remote(
                wall.at[w, slot],
                wall.at[w, slot],
                xsend_sem.at[w],
                xrecv_sem.at[w, plane],
                at_plane(i),
            ).start()
            return 0

        lax.fori_loop(1, NX, send_plane, 0)
        remote(wall.at[w, slot], wall.at[w, slot], csend_sem.at[w], crecv_sem.at[w], sibling).start()

    def pass_on(w):
        def one(i, _):
            p = lax.rem(plane + NX - i, NX)
            s = ((p // NJ) * 2 + core) * NJ + p % NJ
            taken(wall.at[w, s], xrecv_sem.at[w, p])
            remote(wall.at[w, s], wall.at[w, s], csend_sem.at[w], crecv_sem.at[w], sibling).start()
            return 0

        lax.fori_loop(1, NX, one, 0)

    def assemble(w):
        taken(wall.at[w, pl.ds(0, NX)], crecv_sem.at[w])
        for u in range(NSEC):
            stacked = wall[w, u * NJ : (u + 1) * NJ].reshape(D, D)
            mats[w, u] = nn(perm[0], stacked).astype(BF16)

    pass_on(0)
    assemble(0)

    taken(right, load_sem.at[0])

    def source(k):
        u = sec - shift_ref[k]
        inside = (u >= 0) & (u < NSEC)
        return jnp.clip(u, 0, NSEC - 1), inside

    for k in range(NPAIR):
        u, inside = source(k)
        weight = scale_ref[orb_ref[k, 0]] * scale_ref[orb_ref[k, 1]] * SCALE
        weight = jnp.where(inside, weight, 0.0)
        carried[k] = (weight * nt(mats[0, u], right[k])).astype(BF16)

    pass_on(1)

    taken(left, load_sem.at[1])
    total = nn(left[0], carried[0])
    for k in range(1, NPAIR):
        total += nn(left[k], carried[k])
    for h in range(2):
        sig[h] = total[:, h * H : (h + 1) * H]

    for t in range(NJ):
        for h in range(2):
            for r in range(2):
                rs_send[t, 2 * h + r] = sig[h, pl.ds(2 * t + r, 16, stride=16), :].astype(rs_send.dtype)

    def send_rs(i, _):
        t = lax.rem(j + i, NJ)
        remote(
            rs_send.at[t], rs_recv.at[j], rsend_sem, rrecv_sem, {"ops": z * NJ + t, "sec": sec}
        ).start()
        return 0

    lax.fori_loop(1, NJ, send_rs, 0)
    rs_recv[j] = rs_send[j]

    own_wave = mats[0, sec]
    ham_rows = nn(ham_ref[0], own_wave)
    num = jnp.sum(ham_rows * masked_rows, axis=0, keepdims=True)
    for h in range(2):
        num_h = jnp.sum(sig[h] * own_wave[:, h * H : (h + 1) * H].astype(F32), axis=0, keepdims=True)
        part = num_h + num[:, h * H : (h + 1) * H]
        lanes = part if h == 0 else lanes + part
    corr_own[...] = lanes
    remote(corr_own, corr_sib, ksend_sem, krecv_sem, sibling).start()

    assemble(1)
    basis_t[...] = nt(perm[1], mats[1, sec]).astype(BF16)

    taken(corr_sib, krecv_sem)
    corr_x[plane] = corr_own[...] + corr_sib[...]

    def send_corr(i, _):
        remote(corr_x.at[plane], corr_x.at[plane], qsend_sem, qrecv_sem, at_plane(i)).start()
        return 0

    lax.fori_loop(1, NX, send_corr, 0)

    def renormalize(ks):
        for k in ks:
            u, inside = source(k)
            left_basis = nn(left[k], mats[1, u]).astype(BF16)
            value = nn(basis_t[...], left_basis)
            renorm[k] = jnp.where(inside, value, 0.0).astype(BF16)
            pltpu.make_async_copy(renorm.at[k], renorm_hbm.at[0, k], out_sem).start()

    renormalize(range(NPAIR // 2))

    taken(rs_recv.at[pl.ds(0, NJ - 1)], rrecv_sem)
    chunk = [rs_recv[0, q].astype(F32) for q in range(4)]
    for t in range(1, NJ):
        for q in range(4):
            chunk[q] += rs_recv[t, q].astype(F32)
    for q in range(4):
        zs_send[:, q, :] = chunk[q]
    taken(corr_x.at[pl.ds(0, NX - 1)], qrecv_sem)
    zs_send[:, 4:8, :] = jnp.broadcast_to(jnp.sum(corr_x[...], axis=0, keepdims=True), (NZ, 4, H))

    def send_sum(i, _):
        t = lax.rem(z + i, NZ)
        remote(zs_send.at[t], zs_recv.at[z], ssend_sem, srecv_sem, at_z(i)).start()
        return 0

    lax.fori_loop(1, NZ, send_sum, 0)
    zs_recv[z] = zs_send[z]

    renormalize(range(NPAIR // 2, NPAIR))

    norm = jnp.zeros((D, D), F32)
    for u in range(NSEC):
        wide = mats[0, u].astype(F32)
        norm += wide * wide
    norm = jnp.sum(jnp.sum(norm, axis=0, keepdims=True), axis=1, keepdims=True)

    taken(zs_recv.at[pl.ds(0, NZ - 1)], srecv_sem)
    summed = jnp.sum(zs_recv[...], axis=0)
    energy = jnp.sum(summed[4:5, :], axis=1, keepdims=True) / norm
    for h in range(2):
        rows = summed[2 * h : 2 * h + 2, :] + ham_rows[:, h * H : (h + 1) * H]
        resid_ref[0, :, h * H : (h + 1) * H] = rows - energy * masked_rows[:, h * H : (h + 1) * H]

    for w in range(2):
        taken(zbuf.at[w, pl.ds(0, NZ - 1)], zsend_sem.at[w])
        taken(wall.at[w, pl.ds(0, NX - 1)], xsend_sem.at[w])
        taken(wall.at[w, pl.ds(0, NX)], csend_sem.at[w])
    taken(rs_send.at[pl.ds(0, NJ - 1)], rsend_sem)
    taken(corr_own, ksend_sem)
    taken(corr_x.at[pl.ds(0, NX - 1)], qsend_sem)
    taken(zs_send.at[pl.ds(0, NZ - 1)], ssend_sem)
    pltpu.make_async_copy(renorm, renorm_hbm.at[0], out_sem).wait()


RS_TYPE = BF16


def on_device(
    wave,
    sector_live,
    left_ops,
    right_ops,
    pair_shift,
    pair_orbitals,
    orbital_scale,
    block_ham,
    site_basis,
):
    smem = pl.BlockSpec(memory_space=pltpu.SMEM)
    vmem = pl.BlockSpec(memory_space=pltpu.VMEM)
    hbm = pl.BlockSpec(memory_space=pl.ANY)
    dma = pltpu.SemaphoreType.DMA
    return pl.pallas_call(
        kernel,
        out_shape=(
            jax.ShapeDtypeStruct((1, 2, D), F32),
            jax.ShapeDtypeStruct((1, NPAIR, D, D), BF16),
        ),
        in_specs=[smem] * 4 + [vmem] * 3 + [hbm] * 2,
        out_specs=(vmem, hbm),
        scratch_shapes=[
            pltpu.VMEM((NPAIR, D, D), BF16),
            pltpu.VMEM((NPAIR, D, D), BF16),
            pltpu.VMEM((NPAIR, D, D), BF16),
            pltpu.VMEM((NPAIR, D, D), BF16),
            pltpu.VMEM((2, NZ, 4, H), F32),
            pltpu.VMEM((2, NSEC * NJ, 32, D), BF16),
            pltpu.VMEM((2, NSEC, D, D), BF16),
            pltpu.VMEM((2, D, D), BF16),
            pltpu.VMEM((D, D), BF16),
            pltpu.VMEM((2, D, H), F32),
            pltpu.VMEM((NJ, 4, NZ, H), RS_TYPE),
            pltpu.VMEM((NJ, 4, NZ, H), RS_TYPE),
            pltpu.VMEM((1, H), F32),
            pltpu.VMEM((1, H), F32),
            pltpu.VMEM((NX, 1, H), F32),
            pltpu.VMEM((NZ, 8, H), F32),
            pltpu.VMEM((NZ, 8, H), F32),
            dma((2,)),
            dma,
            dma((2,)),
            dma((2,)),
            dma((2,)),
            dma((2, NX)),
            dma((2,)),
            dma((2,)),
            dma,
            dma,
            dma,
            dma,
            dma,
            dma,
            dma,
            dma,
        ],
        compiler_params=pltpu.CompilerParams(
            collective_id=0, has_side_effects=True, vmem_limit_bytes=48 * 1024 * 1024
        ),
        cost_estimate=pl.CostEstimate(flops=1900000000, bytes_accessed=4800000, transcendentals=0),
    )(
        sector_live,
        pair_shift,
        pair_orbitals,
        orbital_scale,
        wave,
        block_ham,
        site_basis,
        left_ops,
        right_ops,
    )


def solution(mesh):
    placed = (
        P("sec", "ops", None),
        P("sec"),
        P("sec", "ops", None, None),
        P("sec", "ops", None, None),
        P("ops"),
        P("ops", None),
        P(),
        P("sec", "ops", None),
        P("sec", "ops", None),
    )
    return jax.shard_map(
        on_device,
        mesh=mesh,
        in_specs=placed,
        out_specs=(P("sec", "ops", None), P("sec", "ops", None, None)),
        check_vma=False,
    )
```

time: 1740 us -> 65.6 us (0.04)
  waiting for transfers between devices: 1250 us -> 0 us
  blocking collectives: 448 us -> 0 us
  Pallas kernels: 0 us -> 55.4 us
    unnamed x3 -> x0, waiting for transfers between devices: 1180 us -> none
    all_gather x1 -> x0, blocking collectives: 310 us -> none  [fetch_rows(): return lax.all_gather(stacked, 'ops', axis=1, tiled=True)]
    psum x1 -> x0, blocking collectives: 139 us -> none  [on_device(): lax.psum((jnp.sum(masked_wide * sigma), jnp.sum(masked_wide * masked_wide...]
    all_gather x1 -> x0, waiting for transfers between devices: 71.6 us -> none  [fetch_sectors(): return lax.all_gather(stacked, 'sec', axis=0, tiled=True)]
    pallas_call x0 -> x1, Pallas kernels: none -> 55.4 us  [on_device(): pl.pallas_call(kernel, out_shape=(jax.ShapeDtypeStruct((1, 2, D), F32), j...]
  transfers between devices with their start and end apart: 2 -> 0, of which waited for: 2 -> 0; matrix products, arithmetic and copies ran while one was open for 1% -> 0% of each run, Pallas kernels for 0% -> 0%
where the time goes in v1:
time: 65.6 us; the launch traced here: 65.3 us
  Pallas kernels  55.4 us (84%)
  local copies, waits for them, and re-layouts  8.65 us (13%)
  between operations  1.29 us (2%)
    pallas_call x1, Pallas kernels, on_device(): pl.pallas_call(kernel, out_shape=(jax.ShapeDtypeStruct((1, 2, D), F32), j...  55.4 us
    unnamed x17, local copies, waits for them, and re-layouts  8.65 us

profile of v1, /device:TPU:1, one launch (start us, length us, event | category | flops | bytes accessed | tf_op | source)
XLA Modules:
  0.0 65.3 jit_solution(12606514701856566550)
XLA Ops:
  1.3 0.8 %copy.11.orb_ref = s32[12,2]{1,0:T(8,128)S(1)} copy(s32[12,2]{0,1:T(2,128)} %param.14) | data formatting | bytes 192 | tf_op args[5]
  2.0 0.0 copy-start
  2.0 1.4 %copy-done = bf16[1,12,256,256]{3,2,1,0:T(8,128)(2,1)S(1)} copy-done((bf16[1,12,256,256]{3,2,1,0:T(8,128)(2,1)S(1)}, bf16[1,12,256,256]{3,2,1,0:T(8,128)(2,1)}, u32[]{:S(2)}) %copy-start) | copy-done | bytes 1572888
  3.5 0.0 copy-start.1
  3.5 1.4 %copy-done.1 = bf16[1,12,256,256]{3,2,1,0:T(8,128)(2,1)S(1)} copy-done((bf16[1,12,256,256]{3,2,1,0:T(8,128)(2,1)S(1)}, bf16[1,12,256,256]{3,2,1,0:T(8,128)(2,1)}, u32[]{:S(2)}) %copy-start.1) | copy-done | bytes 1572888
  4.9 0.0 copy-start.2
  4.9 0.7 %copy-done.2 = bf16[1,2,256]{2,1,0:T(2,128)(2,1)S(1)} copy-done((bf16[1,2,256]{2,1,0:T(2,128)(2,1)S(1)}, bf16[1,2,256]{2,1,0:T(2,128)(2,1)}, u32[]{:S(2)}) %copy-start.2) | copy-done | bytes 1048
  5.5 0.0 copy-start.3
  5.5 0.7 %copy-done.3 = bf16[1,2,256]{2,1,0:T(2,128)(2,1)S(1)} copy-done((bf16[1,2,256]{2,1,0:T(2,128)(2,1)S(1)}, bf16[1,2,256]{2,1,0:T(2,128)(2,1)}, u32[]{:S(2)}) %copy-start.3) | copy-done | bytes 1048
  6.2 0.0 copy-start.4
  6.2 0.7 %copy-done.4 = bf16[1,2,256]{2,1,0:T(2,128)(2,1)S(1)} copy-done((bf16[1,2,256]{2,1,0:T(2,128)(2,1)S(1)}, bf16[1,2,256]{2,1,0:T(2,128)(2,1)}, u32[]{:S(2)}) %copy-start.4) | copy-done | bytes 1048
  6.9 0.0 copy-start.5
  6.9 0.7 %copy-done.5 = s32[12]{0:T(128)S(1)} copy-done((s32[12]{0:T(128)S(1)}, s32[12]{0:T(128)}, u32[]{:S(2)}) %copy-start.5) | copy-done | bytes 72
  7.6 0.0 copy-start.6
  7.6 0.7 %copy-done.6 = f32[120]{0:T(128)S(1)} copy-done((f32[120]{0:T(128)S(1)}, f32[120]{0:T(128)}, u32[]{:S(2)}) %copy-start.6) | copy-done | bytes 504
  8.2 55.4 %shard_map.104 = (f32[1,2,256]{2,1,0:T(2,128)S(1)}, bf16[1,12,256,256]{3,2,1,0:T(8,128)(2,1)S(1)}) custom-call(s32[1]{0:T(128)S(6)} %copy.14.live_ref, s32[12]{0:T(128)S(1)} %copy-done.5, s32[12,2]{1,0:T(8,128)S(1)} %copy.11.orb_ref, f32[120]{0:T(128)S(1)} %copy-done.6, bf16[1,2,256]{2,1,0:T(2,128)(2,1)S(1)} %copy-done.2, bf16[1,2,256]{2,1,0:T(2,128)(2,1)S(1)} %copy-done.3, ...), custom_call_target="tpu_custom_call" | custom-call | flops 1900000000 | bytes 4800000 | tf_op jit(solution)/shard_map/pallas_call | solution.py:320
  63.6 0.6 copy.15
  64.2 1.1 %copy.16 = bf16[1,12,256,256]{3,2,1,0:T(8,128)(2,1)} copy(bf16[1,12,256,256]{3,2,1,0:T(8,128)(2,1)S(1)} %get-tuple-element.5) | data formatting | bytes 3145728
Async XLA Ops:
  2.0 1.4 %copy-start = (bf16[1,12,256,256]{3,2,1,0:T(8,128)(2,1)S(1)}, bf16[1,12,256,256]{3,2,1,0:T(8,128)(2,1)}, u32[]{:S(2)}) copy-start(bf16[1,12,256,256]{3,2,1,0:T(8,128)(2,1)} %left_hbm.1) | copy-start | bytes 4718596
  3.5 1.4 %copy-start.1 = (bf16[1,12,256,256]{3,2,1,0:T(8,128)(2,1)S(1)}, bf16[1,12,256,256]{3,2,1,0:T(8,128)(2,1)}, u32[]{:S(2)}) copy-start(bf16[1,12,256,256]{3,2,1,0:T(8,128)(2,1)} %right_hbm.1) | copy-start | bytes 4718596
  4.9 0.7 %copy-start.2 = (bf16[1,2,256]{2,1,0:T(2,128)(2,1)S(1)}, bf16[1,2,256]{2,1,0:T(2,128)(2,1)}, u32[]{:S(2)}) copy-start(bf16[1,2,256]{2,1,0:T(2,128)(2,1)} %wave_ref.1) | copy-start | bytes 3076
  5.5 0.7 %copy-start.3 = (bf16[1,2,256]{2,1,0:T(2,128)(2,1)S(1)}, bf16[1,2,256]{2,1,0:T(2,128)(2,1)}, u32[]{:S(2)}) copy-start(bf16[1,2,256]{2,1,0:T(2,128)(2,1)} %ham_ref.1) | copy-start | bytes 3076
  6.2 0.7 %copy-start.4 = (bf16[1,2,256]{2,1,0:T(2,128)(2,1)S(1)}, bf16[1,2,256]{2,1,0:T(2,128)(2,1)}, u32[]{:S(2)}) copy-start(bf16[1,2,256]{2,1,0:T(2,128)(2,1)} %basis_ref.1) | copy-start | bytes 3076
  6.9 0.7 %copy-start.5 = (s32[12]{0:T(128)S(1)}, s32[12]{0:T(128)}, u32[]{:S(2)}) copy-start(s32[12]{0:T(128)} %shift_ref.1) | copy-start | bytes 148
  7.6 0.7 %copy-start.6 = (f32[120]{0:T(128)S(1)}, f32[120]{0:T(128)}, u32[]{:S(2)}) copy-start(f32[120]{0:T(128)} %scale_ref.1) | copy-start | bytes 1444

commit v2 on v1

v2 whole, which is shorter than its diff:
```python
import functools
import math

import jax
import jax.numpy as jnp
from jax import lax
from jax.experimental import pallas as pl
from jax.experimental.pallas import tpu as pltpu
from jax.sharding import PartitionSpec as P

MESH = pl.DeviceIdType.MESH
F32 = jnp.float32
BF16 = jnp.bfloat16
NZ = 16
NJ = 8
NX = 16
NSEC = 4
NPAIR = 12
NORB = 120
D = 256
H = 128
SCALE = 1.0 / math.sqrt(256 * 1536)

Z_STEPS = sorted(range(1, NZ), key=lambda i: -min(i, NZ - i))
XY_STEPS = sorted(
    [(a, b) for a in range(4) for b in range(4) if a or b],
    key=lambda s: -(min(s[0], 4 - s[0]) + min(s[1], 4 - s[1])),
)
J_STEPS = sorted(
    [(a, b) for a in range(2) for b in range(4) if a or b],
    key=lambda s: -(2 * s[0] + min(s[1], 4 - s[1])),
)


def nt(a, b):
    return lax.dot_general(a, b, (((1,), (1,)), ((), ())), preferred_element_type=F32)


def nn(a, b):
    return jnp.dot(a, b, preferred_element_type=F32)


def kernel(
    live_hbm,
    shift_hbm,
    orb_hbm,
    scale_hbm,
    wave_hbm,
    ham_hbm,
    basis_hbm,
    left_hbm,
    right_hbm,
    resid_ref,
    renorm_ref,
    live_ref,
    shift_ref,
    orb_ref,
    scale_ref,
    wave_ref,
    ham_ref,
    basis_ref,
    left,
    right,
    carried,
    zbuf,
    wall,
    mats,
    perm,
    basis_t,
    sig,
    rs_send,
    rs_recv,
    corr_own,
    corr_sib,
    corr_x,
    corr_zown,
    corr_z,
    zs_send,
    zs_recv,
    small_sem,
    load_sem,
    zsend_sem,
    zrecv_sem,
    xsend_sem,
    xrecv_sem,
    csend_sem,
    crecv_sem,
    rsend_sem,
    rrecv_sem,
    ksend_sem,
    krecv_sem,
    qsend_sem,
    qrecv_sem,
    ssend_sem,
    srecv_sem,
    tsend_sem,
    trecv_sem,
):
    ops = lax.axis_index("ops")
    sec = lax.axis_index("sec")
    z = ops // NJ
    j = ops % NJ
    x_hi = j // 4
    y = j % 4
    x_lo = sec // 2
    core = sec % 2
    x = x_hi * 2 + x_lo

    def at_z(i):
        return {"ops": ((z + i) % NZ) * NJ + j, "sec": sec}

    def place(a, b):
        px, py = (x + a) % 4, (y + b) % 4
        return (px // 2) * 4 + py, (px % 2) * 2 + core

    def at_plane(step):
        pj, psec = place(*step)
        return {"ops": z * NJ + pj, "sec": psec}

    def plane_slot(step):
        pj, psec = place(*step)
        return psec * NJ + pj

    def at_j(step):
        t = ((x_hi + step[0]) % 2) * 4 + (y + step[1]) % 4
        return t, {"ops": z * NJ + t, "sec": sec}

    sibling = {"ops": ops, "sec": x_lo * 2 + (1 - core)}

    def send(src, dst, send_sem, recv_sem, device):
        pltpu.make_async_remote_copy(
            src_ref=src,
            dst_ref=dst,
            send_sem=send_sem,
            recv_sem=recv_sem,
            device_id=device,
            device_id_type=MESH,
        ).start()

    def taken(ref, sem):
        pltpu.make_async_copy(ref, ref, sem).wait()

    sent = []

    def owe(ref, sem):
        sent.append(lambda: taken(ref, sem))

    barrier = pltpu.get_barrier_semaphore()
    for i in Z_STEPS:
        pl.semaphore_signal(barrier, inc=1, device_id=at_z(i), device_id_type=MESH)
    for step in XY_STEPS:
        pl.semaphore_signal(barrier, inc=1, device_id=at_plane(step), device_id_type=MESH)
    pl.semaphore_signal(barrier, inc=1, device_id=sibling, device_id_type=MESH)

    rows_in = (
        pltpu.make_async_copy(live_hbm, live_ref, small_sem.at[0]),
        pltpu.make_async_copy(wave_hbm, wave_ref, small_sem.at[1]),
        pltpu.make_async_copy(basis_hbm, basis_ref, small_sem.at[2]),
    )
    pairs_in = (
        pltpu.make_async_copy(ham_hbm, ham_ref, small_sem.at[3]),
        pltpu.make_async_copy(shift_hbm, shift_ref, small_sem.at[4]),
        pltpu.make_async_copy(orb_hbm, orb_ref, small_sem.at[5]),
        pltpu.make_async_copy(scale_hbm, scale_ref, small_sem.at[6]),
        pltpu.make_async_copy(right_hbm.at[0], right, load_sem.at[0]),
    )
    left_in = pltpu.make_async_copy(left_hbm.at[0], left, load_sem.at[1])
    for copy in rows_in + pairs_in + (left_in,):
        copy.start()

    m_ids = lax.broadcasted_iota(jnp.int32, (D, D), 0)
    s_ids = lax.broadcasted_iota(jnp.int32, (D, D), 1)
    wanted = ((m_ids % 16) // 2) * 32 + (m_ids % 2) * 16 + m_ids // 16
    perm[0] = jnp.where(wanted == s_ids, 1.0, 0.0).astype(BF16)
    perm[1] = jnp.where(m_ids == s_ids, 1.0, 0.0).astype(BF16)

    for copy in rows_in:
        copy.wait()
    live = live_ref[0, 0]
    row_ids = ops * 2 + lax.broadcasted_iota(jnp.int32, (2, D), 0)
    col_ids = lax.broadcasted_iota(jnp.int32, (2, D), 1)
    keep = (row_ids < live) & (col_ids < live)
    masked_rows = jnp.where(keep, wave_ref[0].astype(F32), 0.0)
    basis_rows = basis_ref[0].astype(F32)
    for w, rows in enumerate((masked_rows, basis_rows)):
        zbuf[w, z] = jnp.concatenate([rows[:, :H], rows[:, H:]], axis=0).astype(BF16)

    pl.semaphore_wait(barrier, (NZ - 1) + (NX - 1) + 1)

    for w in range(2):
        for i in Z_STEPS:
            send(zbuf.at[w, z], zbuf.at[w, z], zsend_sem.at[w], zrecv_sem.at[w], at_z(i))
        owe(zbuf.at[w, pl.ds(0, NZ - 1)], zsend_sem.at[w])

    slot = sec * NJ + j
    for w in range(2):
        taken(zbuf.at[w, pl.ds(0, NZ - 1)], zrecv_sem.at[w])
        pieces = zbuf[w].astype(F32)
        for h in range(2):
            for r in range(2):
                wall[w, slot, r * 16 : (r + 1) * 16, h * H : (h + 1) * H] = pieces[:, 2 * h + r, :].astype(BF16)
        for n, step in enumerate(XY_STEPS):
            send(
                wall.at[w, slot],
                wall.at[w, slot],
                xsend_sem.at[w],
                xrecv_sem.at[w, n],
                at_plane(step),
            )
        owe(wall.at[w, pl.ds(0, NX - 1)], xsend_sem.at[w])
        send(wall.at[w, slot], wall.at[w, slot], csend_sem.at[w], crecv_sem.at[w], sibling)

    def pass_on(w):
        for n in reversed(range(NX - 1)):
            a, b = XY_STEPS[n]
            s = plane_slot((4 - a, 4 - b))
            taken(wall.at[w, s], xrecv_sem.at[w, n])
            send(wall.at[w, s], wall.at[w, s], csend_sem.at[w], crecv_sem.at[w], sibling)
        owe(wall.at[w, pl.ds(0, NX)], csend_sem.at[w])

    def assemble(w):
        taken(wall.at[w, pl.ds(0, NX)], crecv_sem.at[w])
        for u in range(NSEC):
            stacked = wall[w, u * NJ : (u + 1) * NJ].reshape(D, D)
            mats[w, u] = nn(perm[0], stacked).astype(BF16)

    pass_on(0)
    assemble(0)

    for copy in pairs_in:
        copy.wait()

    def source(k):
        u = sec - shift_ref[k]
        inside = (u >= 0) & (u < NSEC)
        return jnp.clip(u, 0, NSEC - 1), inside

    for k in range(NPAIR):
        u, inside = source(k)
        weight = scale_ref[orb_ref[0, k]] * scale_ref[orb_ref[1, k]] * SCALE
        weight = jnp.where(inside, weight, 0.0)
        carried[k] = (weight * nt(mats[0, u], right[k])).astype(BF16)

    left_in.wait()
    total = nn(left[0], carried[0])
    for k in range(1, NPAIR):
        total += nn(left[k], carried[k])
    for h in range(2):
        sig[h] = total[:, h * H : (h + 1) * H]

    for t in range(NJ):
        for h in range(2):
            for r in range(2):
                rs_send[t, 2 * h + r] = sig[h, pl.ds(2 * t + r, 16, stride=16), :].astype(BF16)
    for step in J_STEPS:
        t, device = at_j(step)
        send(rs_send.at[t], rs_recv.at[j], rsend_sem, rrecv_sem, device)
    owe(rs_send.at[pl.ds(0, NJ - 1)], rsend_sem)
    rs_recv[j] = rs_send[j]

    own_wave = mats[0, sec]
    ham_rows = nn(ham_ref[0], own_wave)
    num = jnp.sum(ham_rows * masked_rows, axis=0, keepdims=True)
    lanes = num[:, :H] + num[:, H:]
    for h in range(2):
        wide = own_wave[:, h * H : (h + 1) * H].astype(F32)
        lanes += jnp.sum(sig[h] * wide, axis=0, keepdims=True)
    corr_own[...] = lanes
    send(corr_own, corr_sib, ksend_sem, krecv_sem, sibling)
    owe(corr_own, ksend_sem)

    pass_on(1)

    taken(corr_sib, krecv_sem)
    corr_x[x_lo * NJ + j] = corr_own[...] + corr_sib[...]
    for step in XY_STEPS:
        mine = corr_x.at[x_lo * NJ + j]
        send(mine, mine, qsend_sem, qrecv_sem, at_plane(step))
    owe(corr_x.at[pl.ds(0, NX - 1)], qsend_sem)

    assemble(1)
    basis_t[...] = nt(perm[1], mats[1, sec]).astype(BF16)

    def renormalize(ks):
        for k in ks:
            u, inside = source(k)
            left_basis = nn(left[k], mats[1, u]).astype(BF16)
            value = nn(basis_t[...], left_basis)
            renorm_ref[0, k] = jnp.where(inside, value, 0.0).astype(BF16)

    renormalize(range(NPAIR // 2))

    taken(rs_recv.at[pl.ds(0, NJ - 1)], rrecv_sem)
    chunk = [rs_recv[0, q].astype(F32) for q in range(4)]
    for t in range(1, NJ):
        for q in range(4):
            chunk[q] += rs_recv[t, q].astype(F32)
    for q in range(4):
        zs_send[:, q, :] = chunk[q]
    for i in Z_STEPS:
        send(zs_send.at[(z + i) % NZ], zs_recv.at[z], ssend_sem, srecv_sem, at_z(i))
    owe(zs_send.at[pl.ds(0, NZ - 1)], ssend_sem)

    taken(corr_x.at[pl.ds(0, NX - 1)], qrecv_sem)
    corr_zown[...] = jnp.sum(corr_x[...], axis=0)
    for i in Z_STEPS:
        send(corr_zown, corr_z.at[z], tsend_sem, trecv_sem, at_z(i))
    owe(corr_z.at[pl.ds(0, NZ - 1)], tsend_sem)
    zs_recv[z] = zs_send[z]
    corr_z[z] = corr_zown[...]

    renormalize(range(NPAIR // 2, NPAIR))

    norm = jnp.zeros((D, D), F32)
    for u in range(NSEC):
        wide = mats[0, u].astype(F32)
        norm += wide * wide
    norm = jnp.sum(jnp.sum(norm, axis=0, keepdims=True), axis=1, keepdims=True)

    taken(zs_recv.at[pl.ds(0, NZ - 1)], srecv_sem)
    summed = jnp.sum(zs_recv[...], axis=0)
    taken(corr_z.at[pl.ds(0, NZ - 1)], trecv_sem)
    energy = jnp.sum(jnp.sum(corr_z[...], axis=0), axis=1, keepdims=True) / norm
    for h in range(2):
        rows = summed[2 * h : 2 * h + 2, :] + ham_rows[:, h * H : (h + 1) * H]
        resid_ref[0, :, h * H : (h + 1) * H] = rows - energy * masked_rows[:, h * H : (h + 1) * H]

    for wait in sent:
        wait()


def on_device(
    wave,
    sector_live,
    left_ops,
    right_ops,
    pair_shift,
    pair_orbitals,
    orbital_scale,
    block_ham,
    site_basis,
):
    vmem = pl.BlockSpec(memory_space=pltpu.VMEM)
    hbm = pl.BlockSpec(memory_space=pltpu.HBM)
    dma = pltpu.SemaphoreType.DMA

    def in_hbm(value):
        return pltpu.with_memory_space_constraint(value, pltpu.HBM)

    return pl.pallas_call(
        kernel,
        out_shape=(
            jax.ShapeDtypeStruct((1, 2, D), F32),
            jax.ShapeDtypeStruct((1, NPAIR, D, D), BF16),
        ),
        in_specs=[hbm] * 9,
        out_specs=(vmem, vmem),
        scratch_shapes=[
            pltpu.SMEM((1, 1), jnp.int32),
            pltpu.SMEM((NPAIR,), jnp.int32),
            pltpu.SMEM((2, NPAIR), jnp.int32),
            pltpu.SMEM((NORB,), F32),
            pltpu.VMEM((1, 2, D), BF16),
            pltpu.VMEM((1, 2, D), BF16),
            pltpu.VMEM((1, 2, D), BF16),
            pltpu.VMEM((NPAIR, D, D), BF16),
            pltpu.VMEM((NPAIR, D, D), BF16),
            pltpu.VMEM((NPAIR, D, D), BF16),
            pltpu.VMEM((2, NZ, 4, H), BF16),
            pltpu.VMEM((2, NSEC * NJ, 32, D), BF16),
            pltpu.VMEM((2, NSEC, D, D), BF16),
            pltpu.VMEM((2, D, D), BF16),
            pltpu.VMEM((D, D), BF16),
            pltpu.VMEM((2, D, H), F32),
            pltpu.VMEM((NJ, 4, NZ, H), BF16),
            pltpu.VMEM((NJ, 4, NZ, H), BF16),
            pltpu.VMEM((1, H), F32),
            pltpu.VMEM((1, H), F32),
            pltpu.VMEM((NX, 1, H), F32),
            pltpu.VMEM((1, H), F32),
            pltpu.VMEM((NZ, 1, H), F32),
            pltpu.VMEM((NZ, 4, H), F32),
            pltpu.VMEM((NZ, 4, H), F32),
            dma((7,)),
            dma((2,)),
            dma((2,)),
            dma((2,)),
            dma((2,)),
            dma((2, NX)),
            dma((2,)),
            dma((2,)),
            dma,
            dma,
            dma,
            dma,
            dma,
            dma,
            dma,
            dma,
            dma,
            dma,
        ],
        compiler_params=pltpu.CompilerParams(
            collective_id=0, has_side_effects=True, vmem_limit_bytes=48 * 1024 * 1024
        ),
        cost_estimate=pl.CostEstimate(flops=1900000000, bytes_accessed=4800000, transcendentals=0),
    )(
        sector_live.reshape(1, 1),
        in_hbm(pair_shift),
        in_hbm(pair_orbitals.T),
        in_hbm(orbital_scale),
        in_hbm(wave),
        in_hbm(block_ham),
        in_hbm(site_basis),
        in_hbm(left_ops),
        in_hbm(right_ops),
    )


def solution(mesh):
    placed = (
        P("sec", "ops", None),
        P("sec"),
        P("sec", "ops", None, None),
        P("sec", "ops", None, None),
        P("ops"),
        P("ops", None),
        P(),
        P("sec", "ops", None),
        P("sec", "ops", None),
    )
    return jax.shard_map(
        on_device,
        mesh=mesh,
        in_specs=placed,
        out_specs=(P("sec", "ops", None), P("sec", "ops", None, None)),
        check_vma=False,
    )
```

time: 65.6 us -> 48.3 us (0.74)
  Pallas kernels: 55.4 us -> 45.2 us
  local copies, waits for them, and re-layouts: 8.65 us -> 1.72 us
    pallas_call x1, Pallas kernels: 55.4 us -> 45.2 us  [on_device(): pl.pallas_call(kernel, out_shape=(jax.ShapeDtypeStruct((1, 2, D), F32), j...]
    unnamed x17 -> x2, local copies, waits for them, and re-layouts: 8.65 us -> 1.72 us
where the time goes in v2:
time: 48.3 us; the launch traced here: 48.2 us
  Pallas kernels  45.2 us (94%)
  local copies, waits for them, and re-layouts  1.72 us (4%)
  between operations  1.29 us (3%)
    pallas_call x1, Pallas kernels, on_device(): pl.pallas_call(kernel, out_shape=(jax.ShapeDtypeStruct((1, 2, D), F32), j...  45.2 us
    unnamed x2, local copies, waits for them, and re-layouts  1.72 us

profile of v2, /device:TPU:1, one launch (start us, length us, event | category | flops | bytes accessed | tf_op | source)
XLA Modules:
  0.0 48.2 jit_solution(8612470894023682515)
XLA Ops:
  1.3 45.2 %shard_map.104 = (f32[1,2,256]{2,1,0:T(2,128)S(1)}, bf16[1,12,256,256]{3,2,1,0:T(8,128)(2,1)S(1)}) custom-call(s32[1,1]{1,0:T(1,128)} %bitcast.2.live_hbm, s32[12]{0:T(128)} %shift_hbm.1, s32[2,12]{1,0:T(2,128)} %bitcast.3, f32[120]{0:T(128)} %scale_hbm.1, bf16[1,2,256]{2,1,0:T(2,128)(2,1)} %wave_hbm.1, bf16[1,2,256]{2,1,0:T(2,128)(2,1)} %ham_hbm.1, ...), custom_call_target="tpu_custom_call" | custom-call | flops 1900000000 | bytes 4800000 | tf_op jit(solution)/shard_map/pallas_call | solution.py:350
  46.5 0.6 %copy.14 = f32[1,2,256]{2,1,0:T(2,128)} copy(f32[1,2,256]{2,1,0:T(2,128)S(1)} %get-tuple-element.4) | data formatting | bytes 4096
  47.0 1.1 %copy.15 = bf16[1,12,256,256]{3,2,1,0:T(8,128)(2,1)} copy(bf16[1,12,256,256]{3,2,1,0:T(8,128)(2,1)S(1)} %get-tuple-element.5) | data formatting | bytes 3145728

commit v3 on v2

--- a/solution.py
+++ b/solution.py
@@ -20,6 +20,9 @@
 D = 256
 H = 128
 SCALE = 1.0 / math.sqrt(256 * 1536)
+
+NEAR = 4
+DIRECT = {(0, 0): 1, (0, 1): 1, (1, 0): 1, (1, 1): 1}
 
 Z_STEPS = sorted(range(1, NZ), key=lambda i: -min(i, NZ - i))
 XY_STEPS = sorted(
@@ -63,15 +66,14 @@
     right,
     carried,
     zbuf,
-    wall,
-    mats,
+    wall_wave,
+    wall_basis,
+    mine,
     perm,
     basis_t,
     sig,
     rs_send,
     rs_recv,
-    corr_own,
-    corr_sib,
     corr_x,
     corr_zown,
     corr_z,
@@ -82,13 +84,12 @@
     zsend_sem,
     zrecv_sem,
     xsend_sem,
+    osend_sem,
     xrecv_sem,
     csend_sem,
     crecv_sem,
     rsend_sem,
     rrecv_sem,
-    ksend_sem,
-    krecv_sem,
     qsend_sem,
     qrecv_sem,
     ssend_sem,
@@ -96,6 +97,7 @@
     tsend_sem,
     trecv_sem,
 ):
+    walls = (wall_wave, wall_basis)
     ops = lax.axis_index("ops")
     sec = lax.axis_index("sec")
     z = ops // NJ
@@ -117,9 +119,9 @@
         pj, psec = place(*step)
         return {"ops": z * NJ + pj, "sec": psec}
 
-    def plane_slot(step):
+    def at_plane_other(step):
         pj, psec = place(*step)
-        return psec * NJ + pj
+        return {"ops": z * NJ + pj, "sec": psec + 1 - 2 * core}
 
     def at_j(step):
         t = ((x_hi + step[0]) % 2) * 4 + (y + step[1]) % 4
@@ -146,11 +148,11 @@
         sent.append(lambda: taken(ref, sem))
 
     barrier = pltpu.get_barrier_semaphore()
-    for i in Z_STEPS:
-        pl.semaphore_signal(barrier, inc=1, device_id=at_z(i), device_id_type=MESH)
-    for step in XY_STEPS:
-        pl.semaphore_signal(barrier, inc=1, device_id=at_plane(step), device_id_type=MESH)
-    pl.semaphore_signal(barrier, inc=1, device_id=sibling, device_id_type=MESH)
+    greeted = [at_z(i) for d in range(NEAR, 0, -1) for i in (d, NZ - d)]
+    greeted += [at_plane(step) for step in XY_STEPS] + [sibling]
+    greeted += [at_plane_other(step) for step in XY_STEPS[: max(DIRECT.values())]]
+    for device in greeted:
+        pl.semaphore_signal(barrier, inc=1, device_id=device, device_id_type=MESH)
 
     rows_in = (
         pltpu.make_async_copy(live_hbm, live_ref, small_sem.at[0]),
@@ -169,10 +171,11 @@
         copy.start()
 
     m_ids = lax.broadcasted_iota(jnp.int32, (D, D), 0)
-    s_ids = lax.broadcasted_iota(jnp.int32, (D, D), 1)
-    wanted = ((m_ids % 16) // 2) * 32 + (m_ids % 2) * 16 + m_ids // 16
-    perm[0] = jnp.where(wanted == s_ids, 1.0, 0.0).astype(BF16)
-    perm[1] = jnp.where(m_ids == s_ids, 1.0, 0.0).astype(BF16)
+    g_ids = lax.broadcasted_iota(jnp.int32, (D, D), 1)
+    s_ids = lax.rem(m_ids // 16 + (NZ + NEAR) - z, NZ)
+    wanted = (s_ids // 8) * 128 + ((m_ids % 16) // 2) * 16 + (m_ids % 2) * 8 + s_ids % 8
+    perm[0] = jnp.where(wanted == g_ids, 1.0, 0.0).astype(BF16)
+    perm[1] = jnp.where(m_ids == g_ids, 1.0, 0.0).astype(BF16)
 
     for copy in rows_in:
         copy.wait()
@@ -183,49 +186,79 @@
     masked_rows = jnp.where(keep, wave_ref[0].astype(F32), 0.0)
     basis_rows = basis_ref[0].astype(F32)
     for w, rows in enumerate((masked_rows, basis_rows)):
-        zbuf[w, z] = jnp.concatenate([rows[:, :H], rows[:, H:]], axis=0).astype(BF16)
-
-    pl.semaphore_wait(barrier, (NZ - 1) + (NX - 1) + 1)
+        zbuf[w, NEAR] = jnp.concatenate([rows[:, :H], rows[:, H:]], axis=0).astype(BF16)
+
+    pl.semaphore_wait(barrier, len(greeted))
 
     for w in range(2):
-        for i in Z_STEPS:
-            send(zbuf.at[w, z], zbuf.at[w, z], zsend_sem.at[w], zrecv_sem.at[w], at_z(i))
+        for d in range(NEAR, 0, -1):
+            send(zbuf.at[w, NEAR], zbuf.at[w, NEAR - d], zsend_sem.at[w], zrecv_sem.at[w, 0], at_z(d))
+            send(zbuf.at[w, NEAR], zbuf.at[w, NEAR + d], zsend_sem.at[w], zrecv_sem.at[w, 0], at_z(NZ - d))
         owe(zbuf.at[w, pl.ds(0, NZ - 1)], zsend_sem.at[w])
 
-    slot = sec * NJ + j
-    for w in range(2):
-        taken(zbuf.at[w, pl.ds(0, NZ - 1)], zrecv_sem.at[w])
-        pieces = zbuf[w].astype(F32)
-        for h in range(2):
-            for r in range(2):
-                wall[w, slot, r * 16 : (r + 1) * 16, h * H : (h + 1) * H] = pieces[:, 2 * h + r, :].astype(BF16)
+    def relay(w):
+        taken(zbuf.at[w, pl.ds(0, 2 * NEAR)], zrecv_sem.at[w, 0])
+        send(
+            zbuf.at[w, pl.ds(5, 4)], zbuf.at[w, pl.ds(9, 4)], zsend_sem.at[w], zrecv_sem.at[w, 1], at_z(NZ - NEAR)
+        )
+        send(
+            zbuf.at[w, pl.ds(1, 3)], zbuf.at[w, pl.ds(13, 3)], zsend_sem.at[w], zrecv_sem.at[w, 1], at_z(NEAR)
+        )
+
+    def spread(w, half):
+        if half == 1:
+            taken(zbuf.at[w, pl.ds(9, 7)], zrecv_sem.at[w, 1])
+        pieces = zbuf[w, 8 * half : 8 * half + 8].astype(F32)
+        rows = [
+            jnp.concatenate([pieces[:, r, :], pieces[:, 2 + r, :]], axis=1) for r in range(2)
+        ]
+        block = walls[w].at[sec, half, j]
+        block[...] = jnp.concatenate(rows, axis=0).astype(BF16)
+        n_direct = DIRECT[w, half]
+        xs, os, cs = xsend_sem.at[w, half], osend_sem.at[w, half], csend_sem.at[w, half]
         for n, step in enumerate(XY_STEPS):
-            send(
-                wall.at[w, slot],
-                wall.at[w, slot],
-                xsend_sem.at[w],
-                xrecv_sem.at[w, n],
-                at_plane(step),
-            )
-        owe(wall.at[w, pl.ds(0, NX - 1)], xsend_sem.at[w])
-        send(wall.at[w, slot], wall.at[w, slot], csend_sem.at[w], crecv_sem.at[w], sibling)
-
-    def pass_on(w):
+            send(block, block, xs, xrecv_sem.at[w, half, n], at_plane(step))
+            if n < n_direct:
+                send(block, block, os, crecv_sem.at[w, half], at_plane_other(step))
+        send(block, block, cs, crecv_sem.at[w, half], sibling)
+        owe(blocks(NX - 1), xs)
+        owe(blocks(n_direct), os)
+        owe(blocks(NX - n_direct), cs)
+
+    def blocks(count):
+        return right.at[0, pl.ds(0, 16 * count)]
+
+    def pass_on(w, half):
         for n in reversed(range(NX - 1)):
             a, b = XY_STEPS[n]
-            s = plane_slot((4 - a, 4 - b))
-            taken(wall.at[w, s], xrecv_sem.at[w, n])
-            send(wall.at[w, s], wall.at[w, s], csend_sem.at[w], crecv_sem.at[w], sibling)
-        owe(wall.at[w, pl.ds(0, NX)], csend_sem.at[w])
-
-    def assemble(w):
-        taken(wall.at[w, pl.ds(0, NX)], crecv_sem.at[w])
-        for u in range(NSEC):
-            stacked = wall[w, u * NJ : (u + 1) * NJ].reshape(D, D)
-            mats[w, u] = nn(perm[0], stacked).astype(BF16)
-
-    pass_on(0)
-    assemble(0)
+            pj, psec = place(4 - a, 4 - b)
+            block = walls[w].at[psec, half, pj]
+            taken(block, xrecv_sem.at[w, half, n])
+            if n >= DIRECT[w, half]:
+                send(block, block, csend_sem.at[w, half], crecv_sem.at[w, half], sibling)
+
+    def passed(w, half):
+        taken(walls[w].at[pl.ds(0, 2), half], crecv_sem.at[w, half])
+
+    def gathered(w, u):
+        return walls[w][u].reshape(D, D)
+
+    relay(0)
+    spread(0, 0)
+    relay(1)
+    spread(1, 0)
+    spread(0, 1)
+    pass_on(0, 0)
+    pass_on(1, 0)
+
+    left_in.wait()
+    for k in range(NPAIR):
+        left[k] = nn(left[k], perm[0]).astype(BF16)
+
+    pass_on(0, 1)
+    spread(1, 1)
+    passed(0, 0)
+    passed(0, 1)
 
     for copy in pairs_in:
         copy.wait()
@@ -239,9 +272,8 @@
         u, inside = source(k)
         weight = scale_ref[orb_ref[0, k]] * scale_ref[orb_ref[1, k]] * SCALE
         weight = jnp.where(inside, weight, 0.0)
-        carried[k] = (weight * nt(mats[0, u], right[k])).astype(BF16)
-
-    left_in.wait()
+        carried[k] = (weight * nt(gathered(0, u), right[k])).astype(BF16)
+
     total = nn(left[0], carried[0])
     for k in range(1, NPAIR):
         total += nn(left[k], carried[k])
@@ -258,37 +290,34 @@
     owe(rs_send.at[pl.ds(0, NJ - 1)], rsend_sem)
     rs_recv[j] = rs_send[j]
 
-    own_wave = mats[0, sec]
+    own_wave = nn(perm[0], gathered(0, sec)).astype(BF16)
     ham_rows = nn(ham_ref[0], own_wave)
     num = jnp.sum(ham_rows * masked_rows, axis=0, keepdims=True)
     lanes = num[:, :H] + num[:, H:]
     for h in range(2):
         wide = own_wave[:, h * H : (h + 1) * H].astype(F32)
         lanes += jnp.sum(sig[h] * wide, axis=0, keepdims=True)
-    corr_own[...] = lanes
-    send(corr_own, corr_sib, ksend_sem, krecv_sem, sibling)
-    owe(corr_own, ksend_sem)
-
-    pass_on(1)
-
-    taken(corr_sib, krecv_sem)
-    corr_x[x_lo * NJ + j] = corr_own[...] + corr_sib[...]
+    place_own = sec * NJ + j
+    corr_x[place_own] = lanes
+    part = corr_x.at[place_own]
     for step in XY_STEPS:
-        mine = corr_x.at[x_lo * NJ + j]
-        send(mine, mine, qsend_sem, qrecv_sem, at_plane(step))
-    owe(corr_x.at[pl.ds(0, NX - 1)], qsend_sem)
-
-    assemble(1)
-    basis_t[...] = nt(perm[1], mats[1, sec]).astype(BF16)
+        send(part, part, qsend_sem, qrecv_sem, at_plane_other(step))
+        send(part, part, qsend_sem, qrecv_sem, at_plane(step))
+    send(part, part, qsend_sem, qrecv_sem, sibling)
+    owe(corr_x.at[pl.ds(0, 2 * NX - 1)], qsend_sem)
 
     def renormalize(ks):
         for k in ks:
             u, inside = source(k)
-            left_basis = nn(left[k], mats[1, u]).astype(BF16)
+            left_basis = nn(left[k], gathered(1, u)).astype(BF16)
             value = nn(basis_t[...], left_basis)
             renorm_ref[0, k] = jnp.where(inside, value, 0.0).astype(BF16)
 
-    renormalize(range(NPAIR // 2))
+    norm = jnp.zeros((D, D), F32)
+    for u in range(NSEC):
+        wide = gathered(0, u).astype(F32)
+        norm += wide * wide
+    norm = jnp.sum(jnp.sum(norm, axis=0, keepdims=True), axis=1, keepdims=True)
 
     taken(rs_recv.at[pl.ds(0, NJ - 1)], rrecv_sem)
     chunk = [rs_recv[0, q].astype(F32) for q in range(4)]
@@ -301,7 +330,7 @@
         send(zs_send.at[(z + i) % NZ], zs_recv.at[z], ssend_sem, srecv_sem, at_z(i))
     owe(zs_send.at[pl.ds(0, NZ - 1)], ssend_sem)
 
-    taken(corr_x.at[pl.ds(0, NX - 1)], qrecv_sem)
+    taken(corr_x.at[pl.ds(0, 2 * NX - 1)], qrecv_sem)
     corr_zown[...] = jnp.sum(corr_x[...], axis=0)
     for i in Z_STEPS:
         send(corr_zown, corr_z.at[z], tsend_sem, trecv_sem, at_z(i))
@@ -309,13 +338,13 @@
     zs_recv[z] = zs_send[z]
     corr_z[z] = corr_zown[...]
 
-    renormalize(range(NPAIR // 2, NPAIR))
-
-    norm = jnp.zeros((D, D), F32)
-    for u in range(NSEC):
-        wide = mats[0, u].astype(F32)
-        norm += wide * wide
-    norm = jnp.sum(jnp.sum(norm, axis=0, keepdims=True), axis=1, keepdims=True)
+    pass_on(1, 1)
+    passed(1, 0)
+    passed(1, 1)
+    mine[...] = nn(perm[0], gathered(1, sec)).astype(BF16)
+    basis_t[...] = nt(perm[1], mine[...]).astype(BF16)
+
+    renormalize(range(NPAIR))
 
     taken(zs_recv.at[pl.ds(0, NZ - 1)], srecv_sem)
     summed = jnp.sum(zs_recv[...], axis=0)
@@ -367,16 +396,15 @@
             pltpu.VMEM((NPAIR, D, D), BF16),
             pltpu.VMEM((NPAIR, D, D), BF16),
             pltpu.VMEM((2, NZ, 4, H), BF16),
-            pltpu.VMEM((2, NSEC * NJ, 32, D), BF16),
-            pltpu.VMEM((2, NSEC, D, D), BF16),
+            pltpu.VMEM((NSEC, 2, NJ, 16, D), BF16),
+            pltpu.VMEM((NSEC, 2, NJ, 16, D), BF16),
+            pltpu.VMEM((D, D), BF16),
             pltpu.VMEM((2, D, D), BF16),
             pltpu.VMEM((D, D), BF16),
             pltpu.VMEM((2, D, H), F32),
             pltpu.VMEM((NJ, 4, NZ, H), BF16),
             pltpu.VMEM((NJ, 4, NZ, H), BF16),
-            pltpu.VMEM((1, H), F32),
-            pltpu.VMEM((1, H), F32),
-            pltpu.VMEM((NX, 1, H), F32),
+            pltpu.VMEM((2 * NX, 1, H), F32),
             pltpu.VMEM((1, H), F32),
             pltpu.VMEM((NZ, 1, H), F32),
             pltpu.VMEM((NZ, 4, H), F32),
@@ -384,13 +412,12 @@
             dma((7,)),
             dma((2,)),
             dma((2,)),
-            dma((2,)),
-            dma((2,)),
-            dma((2, NX)),
-            dma((2,)),
-            dma((2,)),
-            dma,
-            dma,
+            dma((2, 2)),
+            dma((2, 2)),
+            dma((2, 2)),
+            dma((2, 2, NX)),
+            dma((2, 2)),
+            dma((2, 2)),
             dma,
             dma,
             dma,

time: 48.3 us -> 47.6 us (0.986)
  Pallas kernels: 45.2 us -> 44.5 us
    pallas_call x1, Pallas kernels: 45.2 us -> 44.5 us  [on_device(): pl.pallas_call(kernel, out_shape=(jax.ShapeDtypeStruct((1, 2, D), F32), j...]
where the time goes in v3:
time: 47.6 us; the launch traced here: 47.5 us
  Pallas kernels  44.5 us (93%)
  local copies, waits for them, and re-layouts  1.72 us (4%)
  between operations  1.29 us (3%)
    pallas_call x1, Pallas kernels, on_device(): pl.pallas_call(kernel, out_shape=(jax.ShapeDtypeStruct((1, 2, D), F32), j...  44.5 us
    unnamed x2, local copies, waits for them, and re-layouts  1.72 us

profile of v3, /device:TPU:1, one launch (start us, length us, event | category | flops | bytes accessed | tf_op | source)
XLA Modules:
  0.0 47.5 jit_solution(13387567280726533375)
XLA Ops:
  1.3 44.5 %shard_map.104 = (f32[1,2,256]{2,1,0:T(2,128)S(1)}, bf16[1,12,256,256]{3,2,1,0:T(8,128)(2,1)S(1)}) custom-call(s32[1,1]{1,0:T(1,128)} %bitcast.2.live_hbm, s32[12]{0:T(128)} %shift_hbm.1, s32[2,12]{1,0:T(2,128)} %bitcast.3, f32[120]{0:T(128)} %scale_hbm.1, bf16[1,2,256]{2,1,0:T(2,128)(2,1)} %wave_hbm.1, bf16[1,2,256]{2,1,0:T(2,128)(2,1)} %ham_hbm.1, ...), custom_call_target="tpu_custom_call" | custom-call | flops 1900000000 | bytes 4800000 | tf_op jit(solution)/shard_map/pallas_call | solution.py:379
  45.8 0.6 %copy.14 = f32[1,2,256]{2,1,0:T(2,128)} copy(f32[1,2,256]{2,1,0:T(2,128)S(1)} %get-tuple-element.4) | data formatting | bytes 4096
  46.3 1.1 %copy.15 = bf16[1,12,256,256]{3,2,1,0:T(8,128)(2,1)} copy(bf16[1,12,256,256]{3,2,1,0:T(8,128)(2,1)S(1)} %get-tuple-element.5) | data formatting | bytes 3145728

commit v4 on v3

--- a/solution.py
+++ b/solution.py
@@ -64,11 +64,16 @@
     basis_ref,
     left,
     right,
-    carried,
+    left_near,
+    left_far,
+    carried_near,
+    carried_far,
     zbuf,
-    wall_wave,
-    wall_basis,
-    mine,
+    wall_wave_near,
+    wall_wave_far,
+    wall_basis_near,
+    wall_basis_far,
+    mats,
     perm,
     basis_t,
     sig,
@@ -97,7 +102,7 @@
     tsend_sem,
     trecv_sem,
 ):
-    walls = (wall_wave, wall_basis)
+    walls = ((wall_wave_near, wall_wave_far), (wall_basis_near, wall_basis_far))
     ops = lax.axis_index("ops")
     sec = lax.axis_index("sec")
     z = ops // NJ
@@ -212,7 +217,7 @@
         rows = [
             jnp.concatenate([pieces[:, r, :], pieces[:, 2 + r, :]], axis=1) for r in range(2)
         ]
-        block = walls[w].at[sec, half, j]
+        block = walls[w][half].at[sec, j]
         block[...] = jnp.concatenate(rows, axis=0).astype(BF16)
         n_direct = DIRECT[w, half]
         xs, os, cs = xsend_sem.at[w, half], osend_sem.at[w, half], csend_sem.at[w, half]
@@ -232,16 +237,19 @@
         for n in reversed(range(NX - 1)):
             a, b = XY_STEPS[n]
             pj, psec = place(4 - a, 4 - b)
-            block = walls[w].at[psec, half, pj]
+            block = walls[w][half].at[psec, pj]
             taken(block, xrecv_sem.at[w, half, n])
             if n >= DIRECT[w, half]:
                 send(block, block, csend_sem.at[w, half], crecv_sem.at[w, half], sibling)
 
     def passed(w, half):
-        taken(walls[w].at[pl.ds(0, 2), half], crecv_sem.at[w, half])
+        taken(walls[w][half].at[pl.ds(0, 2)], crecv_sem.at[w, half])
+
+    def gathered_half(w, half, u):
+        return walls[w][half][u].reshape(H, D)
 
     def gathered(w, u):
-        return walls[w][u].reshape(D, D)
+        return jnp.concatenate([gathered_half(w, half, u) for half in range(2)], axis=0)
 
     relay(0)
     spread(0, 0)
@@ -253,12 +261,9 @@
 
     left_in.wait()
     for k in range(NPAIR):
-        left[k] = nn(left[k], perm[0]).astype(BF16)
-
-    pass_on(0, 1)
-    spread(1, 1)
-    passed(0, 0)
-    passed(0, 1)
+        columns = nn(left[k], perm[0]).astype(BF16)
+        left_near[:, k * H : (k + 1) * H] = columns[:, :H]
+        left_far[:, k * H : (k + 1) * H] = columns[:, H:]
 
     for copy in pairs_in:
         copy.wait()
@@ -268,17 +273,26 @@
         inside = (u >= 0) & (u < NSEC)
         return jnp.clip(u, 0, NSEC - 1), inside
 
-    for k in range(NPAIR):
-        u, inside = source(k)
-        weight = scale_ref[orb_ref[0, k]] * scale_ref[orb_ref[1, k]] * SCALE
-        weight = jnp.where(inside, weight, 0.0)
-        carried[k] = (weight * nt(gathered(0, u), right[k])).astype(BF16)
-
-    total = nn(left[0], carried[0])
-    for k in range(1, NPAIR):
-        total += nn(left[k], carried[k])
+    def pair_terms(half, left_part, carried_part):
+        for k in range(NPAIR):
+            u, inside = source(k)
+            weight = scale_ref[orb_ref[0, k]] * scale_ref[orb_ref[1, k]] * SCALE
+            weight = jnp.where(inside, weight, 0.0)
+            product = nt(gathered_half(0, half, u), right[k])
+            carried_part[k * H : (k + 1) * H, :] = (weight * product).astype(BF16)
+        return nn(left_part[...], carried_part[...])
+
+    passed(0, 0)
+    total = pair_terms(0, left_near, carried_near)
     for h in range(2):
         sig[h] = total[:, h * H : (h + 1) * H]
+
+    pass_on(0, 1)
+    spread(1, 1)
+    passed(0, 1)
+    total = pair_terms(1, left_far, carried_far)
+    for h in range(2):
+        sig[h] += total[:, h * H : (h + 1) * H]
 
     for t in range(NJ):
         for h in range(2):
@@ -309,7 +323,7 @@
     def renormalize(ks):
         for k in ks:
             u, inside = source(k)
-            left_basis = nn(left[k], gathered(1, u)).astype(BF16)
+            left_basis = nn(left[k], mats[u]).astype(BF16)
             value = nn(basis_t[...], left_basis)
             renorm_ref[0, k] = jnp.where(inside, value, 0.0).astype(BF16)
 
@@ -341,8 +355,9 @@
     pass_on(1, 1)
     passed(1, 0)
     passed(1, 1)
-    mine[...] = nn(perm[0], gathered(1, sec)).astype(BF16)
-    basis_t[...] = nt(perm[1], mine[...]).astype(BF16)
+    for u in range(NSEC):
+        mats[u] = nn(perm[0], gathered(1, u)).astype(BF16)
+    basis_t[...] = nt(perm[1], mats[sec]).astype(BF16)
 
     renormalize(range(NPAIR))
 
@@ -394,11 +409,16 @@
             pltpu.VMEM((1, 2, D), BF16),
             pltpu.VMEM((NPAIR, D, D), BF16),
             pltpu.VMEM((NPAIR, D, D), BF16),
-            pltpu.VMEM((NPAIR, D, D), BF16),
+            pltpu.VMEM((D, NPAIR * H), BF16),
+            pltpu.VMEM((D, NPAIR * H), BF16),
+            pltpu.VMEM((NPAIR * H, D), BF16),
+            pltpu.VMEM((NPAIR * H, D), BF16),
             pltpu.VMEM((2, NZ, 4, H), BF16),
-            pltpu.VMEM((NSEC, 2, NJ, 16, D), BF16),
-            pltpu.VMEM((NSEC, 2, NJ, 16, D), BF16),
-            pltpu.VMEM((D, D), BF16),
+            pltpu.VMEM((NSEC, NJ, 16, D), BF16),
+            pltpu.VMEM((NSEC, NJ, 16, D), BF16),
+            pltpu.VMEM((NSEC, NJ, 16, D), BF16),
+            pltpu.VMEM((NSEC, NJ, 16, D), BF16),
+            pltpu.VMEM((NSEC, D, D), BF16),
             pltpu.VMEM((2, D, D), BF16),
             pltpu.VMEM((D, D), BF16),
             pltpu.VMEM((2, D, H), F32),

time: 47.6 us -> 47.2 us (level)
  Pallas kernels: 44.5 us -> 44 us
where the time goes in v4:
time: 47.2 us; the launch traced here: 47 us
  Pallas kernels  44 us (93%)
  local copies, waits for them, and re-layouts  1.72 us (4%)
  between operations  1.29 us (3%)
    pallas_call x1, Pallas kernels, on_device(): pl.pallas_call(kernel, out_shape=(jax.ShapeDtypeStruct((1, 2, D), F32), j...  44 us
    unnamed x2, local copies, waits for them, and re-layouts  1.72 us

profile of v4, /device:TPU:1, one launch (start us, length us, event | category | flops | bytes accessed | tf_op | source)
XLA Modules:
  0.0 47.0 jit_solution(11541164898719985471)
XLA Ops:
  1.3 44.0 %shard_map.104 = (f32[1,2,256]{2,1,0:T(2,128)S(1)}, bf16[1,12,256,256]{3,2,1,0:T(8,128)(2,1)S(1)}) custom-call(s32[1,1]{1,0:T(1,128)} %bitcast.2.live_hbm, s32[12]{0:T(128)} %shift_hbm.1, s32[2,12]{1,0:T(2,128)} %bitcast.3, f32[120]{0:T(128)} %scale_hbm.1, bf16[1,2,256]{2,1,0:T(2,128)(2,1)} %wave_hbm.1, bf16[1,2,256]{2,1,0:T(2,128)(2,1)} %ham_hbm.1, ...), custom_call_target="tpu_custom_call" | custom-call | flops 1900000000 | bytes 4800000 | tf_op jit(solution)/shard_map/pallas_call | solution.py:394
  45.3 0.6 %copy.14 = f32[1,2,256]{2,1,0:T(2,128)} copy(f32[1,2,256]{2,1,0:T(2,128)S(1)} %get-tuple-element.4) | data formatting | bytes 4096
  45.9 1.1 %copy.15 = bf16[1,12,256,256]{3,2,1,0:T(8,128)(2,1)} copy(bf16[1,12,256,256]{3,2,1,0:T(8,128)(2,1)S(1)} %get-tuple-element.5) | data formatting | bytes 3145728

commit v5 on v4

--- a/solution.py
+++ b/solution.py
@@ -338,8 +338,7 @@
     for t in range(1, NJ):
         for q in range(4):
             chunk[q] += rs_recv[t, q].astype(F32)
-    for q in range(4):
-        zs_send[:, q, :] = chunk[q]
+    zs_send[...] = jnp.stack(chunk, axis=1).astype(BF16)
     for i in Z_STEPS:
         send(zs_send.at[(z + i) % NZ], zs_recv.at[z], ssend_sem, srecv_sem, at_z(i))
     owe(zs_send.at[pl.ds(0, NZ - 1)], ssend_sem)
@@ -362,7 +361,7 @@
     renormalize(range(NPAIR))
 
     taken(zs_recv.at[pl.ds(0, NZ - 1)], srecv_sem)
-    summed = jnp.sum(zs_recv[...], axis=0)
+    summed = jnp.sum(zs_recv[...].astype(F32), axis=0)
     taken(corr_z.at[pl.ds(0, NZ - 1)], trecv_sem)
     energy = jnp.sum(jnp.sum(corr_z[...], axis=0), axis=1, keepdims=True) / norm
     for h in range(2):
@@ -427,8 +426,8 @@
             pltpu.VMEM((2 * NX, 1, H), F32),
             pltpu.VMEM((1, H), F32),
             pltpu.VMEM((NZ, 1, H), F32),
-            pltpu.VMEM((NZ, 4, H), F32),
-            pltpu.VMEM((NZ, 4, H), F32),
+            pltpu.VMEM((NZ, 4, H), BF16),
+            pltpu.VMEM((NZ, 4, H), BF16),
             dma((7,)),
             dma((2,)),
             dma((2,)),

time: 47.2 us -> 47 us (level)
  no operation moved by 1% of the time
where the time goes in v5:
time: 47 us; the launch traced here: 46.9 us
  Pallas kernels  43.8 us (93%)
  local copies, waits for them, and re-layouts  1.72 us (4%)
  between operations  1.29 us (3%)
    pallas_call x1, Pallas kernels, on_device(): pl.pallas_call(kernel, out_shape=(jax.ShapeDtypeStruct((1, 2, D), F32), j...  43.8 us
    unnamed x2, local copies, waits for them, and re-layouts  1.72 us

profile of v5, /device:TPU:1, one launch (start us, length us, event | category | flops | bytes accessed | tf_op | source)
XLA Modules:
  0.0 46.9 jit_solution(3408130871685258998)
XLA Ops:
  1.3 43.8 %shard_map.104 = (f32[1,2,256]{2,1,0:T(2,128)S(1)}, bf16[1,12,256,256]{3,2,1,0:T(8,128)(2,1)S(1)}) custom-call(s32[1,1]{1,0:T(1,128)} %bitcast.2.live_hbm, s32[12]{0:T(128)} %shift_hbm.1, s32[2,12]{1,0:T(2,128)} %bitcast.3, f32[120]{0:T(128)} %scale_hbm.1, bf16[1,2,256]{2,1,0:T(2,128)(2,1)} %wave_hbm.1, bf16[1,2,256]{2,1,0:T(2,128)(2,1)} %ham_hbm.1, ...), custom_call_target="tpu_custom_call" | custom-call | flops 1900000000 | bytes 4800000 | tf_op jit(solution)/shard_map/pallas_call | solution.py:393
  45.1 0.6 %copy.14 = f32[1,2,256]{2,1,0:T(2,128)} copy(f32[1,2,256]{2,1,0:T(2,128)S(1)} %get-tuple-element.4) | data formatting | bytes 4096
  45.7 1.1 %copy.15 = bf16[1,12,256,256]{3,2,1,0:T(8,128)(2,1)} copy(bf16[1,12,256,256]{3,2,1,0:T(8,128)(2,1)S(1)} %get-tuple-element.5) | data formatting | bytes 3145728

commit v6 on v4

--- a/solution.py
+++ b/solution.py
@@ -346,11 +346,16 @@
 
     taken(corr_x.at[pl.ds(0, 2 * NX - 1)], qrecv_sem)
     corr_zown[...] = jnp.sum(corr_x[...], axis=0)
-    for i in Z_STEPS:
-        send(corr_zown, corr_z.at[z], tsend_sem, trecv_sem, at_z(i))
-    owe(corr_z.at[pl.ds(0, NZ - 1)], tsend_sem)
+
+    @pl.when(core == 1)
+    def _():
+        for i in Z_STEPS:
+            send(corr_zown, corr_z.at[z], tsend_sem, trecv_sem, {"ops": at_z(i)["ops"], "sec": sec - 1})
+            send(corr_zown, corr_z.at[z], tsend_sem, trecv_sem, at_z(i))
+        send(corr_zown, corr_z.at[z], tsend_sem, trecv_sem, {"ops": ops, "sec": sec - 1})
+        corr_z[z] = corr_zown[...]
+
     zs_recv[z] = zs_send[z]
-    corr_z[z] = corr_zown[...]
 
     pass_on(1, 1)
     passed(1, 0)
@@ -363,7 +368,15 @@
 
     taken(zs_recv.at[pl.ds(0, NZ - 1)], srecv_sem)
     summed = jnp.sum(zs_recv[...], axis=0)
-    taken(corr_z.at[pl.ds(0, NZ - 1)], trecv_sem)
+
+    @pl.when(core == 0)
+    def _():
+        taken(corr_z, trecv_sem)
+
+    @pl.when(core == 1)
+    def _():
+        taken(corr_z.at[pl.ds(0, NZ - 1)], trecv_sem)
+
     energy = jnp.sum(jnp.sum(corr_z[...], axis=0), axis=1, keepdims=True) / norm
     for h in range(2):
         rows = summed[2 * h : 2 * h + 2, :] + ham_rows[:, h * H : (h + 1) * H]
@@ -371,6 +384,10 @@
 
     for wait in sent:
         wait()
+
+    @pl.when(core == 1)
+    def _():
+        taken(corr_x.at[pl.ds(0, 2 * NX - 1)], tsend_sem)
 
 
 def on_device(

time: 47.2 us -> 47.1 us (level)
  no operation moved by 1% of the time
where the time goes in v6:
time: 47.1 us; the launch traced here: 47 us
  Pallas kernels  44 us (93%)
  local copies, waits for them, and re-layouts  1.72 us (4%)
  between operations  1.29 us (3%)
    pallas_call x1, Pallas kernels, on_device(): pl.pallas_call(kernel, out_shape=(jax.ShapeDtypeStruct((1, 2, D), F32), j...  44 us
    unnamed x2, local copies, waits for them, and re-layouts  1.72 us

profile of v6, /device:TPU:1, one launch (start us, length us, event | category | flops | bytes accessed | tf_op | source)
XLA Modules:
  0.0 47.0 jit_solution(8916686116340144564)
XLA Ops:
  1.3 44.0 %shard_map.104 = (f32[1,2,256]{2,1,0:T(2,128)S(1)}, bf16[1,12,256,256]{3,2,1,0:T(8,128)(2,1)S(1)}) custom-call(s32[1,1]{1,0:T(1,128)} %bitcast.2.live_hbm, s32[12]{0:T(128)} %shift_hbm.1, s32[2,12]{1,0:T(2,128)} %bitcast.3, f32[120]{0:T(128)} %scale_hbm.1, bf16[1,2,256]{2,1,0:T(2,128)(2,1)} %wave_hbm.1, bf16[1,2,256]{2,1,0:T(2,128)(2,1)} %ham_hbm.1, ...), custom_call_target="tpu_custom_call" | custom-call | flops 1900000000 | bytes 4800000 | tf_op jit(solution)/shard_map/pallas_call | solution.py:411
  45.3 0.6 %copy.14 = f32[1,2,256]{2,1,0:T(2,128)} copy(f32[1,2,256]{2,1,0:T(2,128)S(1)} %get-tuple-element.4) | data formatting | bytes 4096
  45.9 1.1 %copy.15 = bf16[1,12,256,256]{3,2,1,0:T(8,128)(2,1)} copy(bf16[1,12,256,256]{3,2,1,0:T(8,128)(2,1)S(1)} %get-tuple-element.5) | data formatting | bytes 3145728
